TPU v7x, 32 devices: a whole 2x2x4 slice. The times are simulated.
32 devices in a mesh: clip: 8 (over z, y), frame: 4 (over x, core).
Axes of the slice: x: 2, y: 2, z: 4, core: 2. Of those that a mesh axis runs over, the one named last changes fastest.
Arguments:
- inputs: bfloat16 [16, 8, 196, 768], P('clip', 'frame'), may hold values from -6 to 6
- out_grad: bfloat16 [16, 8, 196, 768], P('clip', 'frame'), may hold values from -6 to 6
- adapter_index: int32 [16], P('clip'), may hold values from 0 to 7, as said below
- norm_gain: bfloat16 [3, 768], P(None, 'clip'), may hold values from 0.5 to 1.5
- norm_bias: bfloat16 [3, 768], P(None, 'clip'), may hold values from -4 to 4
- qkv_weight: bfloat16 [2, 768, 2304], P(None, 'clip'), may hold values from -0.21875 to 0.21875
- proj_weight: bfloat16 [3, 768, 768], P(None, 'clip'), may hold values from -0.3125 to 0.3125
- mlp_in: bfloat16 [768, 3072], P('clip'), may hold values from -0.21875 to 0.21875
- mlp_out: bfloat16 [3072, 768], P('clip'), may hold values from -0.109375 to 0.109375
- adapt_down: bfloat16 [6, 8, 768, 16], P(None, None, 'clip'), may hold values from -0.21875 to 0.21875
- adapt_down_wide: bfloat16 [8, 3072, 16], P(None, 'clip'), may hold values from -0.109375 to 0.109375
- adapt_up_qkv: bfloat16 [2, 8, 16, 2304], P(None, None, None, 'clip'), may hold values from -1.5 to 1.5
- adapt_up: bfloat16 [4, 8, 16, 768], P(None, None, None, 'clip'), may hold values from -1.5 to 1.5
- adapt_up_wide: bfloat16 [8, 16, 3072], P(None, None, 'clip'), may hold values from -1.5 to 1.5
Outputs:
- output: bfloat16 [16, 8, 196, 768], P('clip', 'frame')
- input_grad: bfloat16 [16, 8, 196, 768], P('clip', 'frame')
- grad_down: float32 [6, 8, 768, 16], P(None, None, 'clip')
- grad_down_wide: float32 [8, 3072, 16], P(None, 'clip')
- grad_up_qkv: float32 [2, 8, 16, 2304], P(None, None, None, 'clip')
- grad_up: float32 [4, 8, 16, 768], P(None, None, None, 'clip')
- grad_up_wide: float32 [8, 16, 3072], P(None, None, 'clip')
Inputs may be any that keep to these rules, and one draw needn't show every extreme that they name: `adapter_index`: every one of the 8 adapters is chosen by at least one clip.
All inputs are finite; a program needn't handle non-finite values.
Results may differ from a plain program's by a relative error of at most 0.025.
Values may be sent and summed in bfloat16 or wider, within the bound.
A program may use at most 256 MiB of HBM per device.

v0:
```python
import functools
import jax
import jax.numpy as jnp
from jax import lax
from jax.experimental import pallas as pl
from jax.experimental.pallas import tpu as pltpu
from jax.sharding import PartitionSpec as P

EPS = 1e-06
MESH = pl.DeviceIdType.MESH
f32 = jnp.float32
bf16 = jnp.bfloat16
D, FF, QKV, RANK = 768, 3072, 2304, 16
NP, GR, R = 196, 208, 832
DOWN = (0, 768, 1536, 2304, 3072, 3840, 4608)
UP = (7680, 12288, 13056, 9984, 13824, 15360, 14592)
ADW = 18432
BIG = 1e30


def dg(a, b, ca, cb):
    return lax.dot_general(a, b, (((ca,), (cb,)), ((), ())), preferred_element_type=f32)


def iota(shape, d):
    return lax.broadcasted_iota(jnp.int32, shape, d)


def cols(off, w):
    return pl.ds(off if isinstance(off, int) else pl.multiple_of(off, 128), w)


def normal_parts(v):
    e = jnp.exp(-0.5 * v * v)
    t = 1.0 / (1.0 + 0.2316419 * jnp.abs(v))
    poly = t * (
        0.127414796
        + t * (-0.142248368 + t * (0.7107068705 + t * (-0.7265760135 + t * 0.5307027145)))
    )
    tail = poly * e
    return jnp.where(v >= 0, 1.0 - tail, tail), e


def onehot(col, width):
    return jnp.where(iota((col.shape[0], width), 1) == col, 1.0, 0.0).astype(bf16)


def message_rows():
    m = iota((GR, 1), 0)
    c = jnp.where(m >= 98, 1, 0)
    rest = m - 98 * c
    f = jnp.where(rest >= 49, 1, 0)
    return m < 196, c, f, rest - 49 * f


def to_message(owner):
    ok, c, f, q = message_rows()
    return jnp.where(ok, (2 * c + f) * GR + 49 * owner + q, -1)


def from_patches(owner):
    ok, c, f, q = message_rows()
    return jnp.where(ok, 392 * c + 8 * q + 2 * owner + f, -1)


def to_patches(chunk):
    t = iota((GR, 1), 0) + chunk * GR
    c = jnp.where(t >= 392, 1, 0)
    u = t - 392 * c
    q, fr = u >> 3, u & 7
    return jnp.where(t < 784, (fr >> 1) * GR + c * 98 + (fr & 1) * 49 + q, -1)


def to_frames(g):
    p = iota((GR, 1), 0)
    d = jnp.where(p >= 49, 1, 0) + jnp.where(p >= 98, 1, 0) + jnp.where(p >= 147, 1, 0)
    return jnp.where(p < NP, d * GR + (g // 2) * 98 + (g % 2) * 49 + p - 49 * d, -1)


def clip_mask(first):
    return (iota((R, 32), 0) >= first) == (iota((R, 32), 1) >= 16)


class Part:
    def __init__(self, ref, c0, width):
        self.ref, self.c0, self.width = ref, c0, width

    def get(self, rows=slice(None), off=0, width=None):
        return self.ref[rows, cols(self.c0 + off, self.width if width is None else width)]

    def put(self, val, rows=slice(None), off=0):
        self.ref[rows, cols(self.c0 + off, val.shape[1])] = val


def chunks(size, body):
    @pl.loop(0, R // size)
    def _(i):
        body(pl.ds(pl.multiple_of(i * size, size), size))


def tiles(total, tile, body, between):
    if total == tile:
        body(0)
    elif between is None:

        @pl.loop(0, total // tile)
        def _(i):
            body(i * tile)

    else:
        for c in range(0, total, tile):
            between(c)
            body(c)


def norm_rows(v):
    mean = jnp.mean(v, axis=-1, keepdims=True)
    cen = v - mean
    rstd = lax.rsqrt(jnp.mean(cen * cen, axis=-1, keepdims=True) + EPS)
    return cen * rstd, rstd


def norm_back_rows(v, gain, dh):
    hat, rstd = norm_rows(v)
    g = dh * gain
    m1 = jnp.mean(g, axis=-1, keepdims=True)
    m2 = jnp.mean(g * hat, axis=-1, keepdims=True)
    return rstd * (g - m1 - hat * m2)


def split_heads(v):
    first = iota(v.shape, 1) < 64
    zero = jnp.zeros(v.shape, bf16)
    return jnp.concatenate([jnp.where(first, v, zero), jnp.where(first, zero, v)], axis=0)


def join_heads(v):
    n = v.shape[0] // 2
    return jnp.where(iota((n, 128), 1) < 64, v[:n], v[n:])


def attend(qkv, rows, n, bias, out, pairs):
    q = [split_heads(qkv.get(rows, o, 128) * bf16(0.125)) for o in pairs]
    s = [dg(a, qkv.get(rows, D + o, 128), 1, 1) + bias for a, o in zip(q, pairs)]
    p = [jnp.exp(a - jnp.max(a, axis=1, keepdims=True)).astype(bf16) for a in s]
    ones = jnp.ones((n, 128), bf16)
    for a, o in zip(p, pairs):
        r = dg(a, jnp.concatenate([qkv.get(rows, 2 * D + o, 128), ones], axis=1), 1, 0)
        out.put(join_heads(r[:, :128] / r[:, 128:]).astype(bf16), rows, o)


def attend_back(qkv, rows, n, bias, dout, pairs, sums_by_product):
    q = [split_heads(qkv.get(rows, o, 128) * bf16(0.125)) for o in pairs]
    k = [qkv.get(rows, D + o, 128) for o in pairs]
    g = [split_heads(dout.get(rows, o, 128)) for o in pairs]
    s = [dg(a, b, 1, 1) + bias for a, b in zip(q, k)]
    dp = [dg(a, qkv.get(rows, 2 * D + o, 128), 1, 1) for a, o in zip(g, pairs)]
    p = [jnp.exp(a - jnp.max(a, axis=1, keepdims=True)) for a in s]
    if sums_by_product:
        ones = jnp.ones((n, n), bf16)
        p = [a * (1.0 / dg(a.astype(bf16), ones, 1, 0)) for a in p]
    else:
        p = [a * (1.0 / jnp.sum(a, axis=1, keepdims=True)) for a in p]
    ds = [(a * (b - jnp.sum(a * b, axis=1, keepdims=True))).astype(bf16) for a, b in zip(p, dp)]
    for i, o in enumerate(pairs):
        qkv.put((join_heads(dg(ds[i], k[i], 1, 0)) * 0.125).astype(bf16), rows, o)
        qkv.put(dg(ds[i], q[i], 0, 0).astype(bf16), rows, D + o)
        qkv.put(dg(p[i].astype(bf16), g[i], 0, 0).astype(bf16), rows, 2 * D + o)


def spatial_loop(count, body):
    bias = jnp.where(iota((1, GR), 1) < NP, 0.0, -BIG)
    steps = 6 // count

    @pl.loop(0, 4 * steps)
    def _(i):
        pairs = [((i % steps) * count + k) * 128 for k in range(count)]
        body(pl.ds(pl.multiple_of((i // steps) * GR, 16), GR), GR, bias, pairs)


def temporal_loop(body):
    pairs = range(0, D, 128)

    def bias(n):
        return jnp.where(((iota((2 * n, n), 0) & (n - 1)) >> 3) == (iota((2 * n, n), 1) >> 3), 0.0, -BIG)

    @pl.loop(0, 6)
    def _(i):
        body(pl.ds(pl.multiple_of(i * 128, 128), 128), 128, bias(128), pairs)

    body(pl.ds(768, 64), 64, bias(64), pairs)


class Many:
    def __init__(self, cps):
        self.cps = cps
        for cp in cps:
            cp.start()

    def wait_recv(self):
        for cp in self.cps:
            cp.wait_recv()

    def wait_send(self):
        for cp in self.cps:
            cp.wait_send()


def gather_groups():
    out = [(f"q0{c}", "q", 0, 0, 96, 16, c, D) for c in range(0, QKV, D)]
    out += [("p0", "p", 0, 0, 96, 16, 0, D), ("p1", "p", 1, 0, 96, 16, 0, D)]
    out += [(f"q1{c}", "q", 1, 0, 96, 16, c, D) for c in range(0, QKV, D)]
    out += [("p2", "p", 2, 0, 96, 16, 0, D)]
    out += [("o", "o", None, r, 96, 16, 0, D) for r in range(0, 384, 96)]
    out += [(f"i{c}", "i", None, 0, 96, 16, c, D) for c in range(0, FF, D)]
    return out


DIRECT = 0
T1, T2, T3 = 2, 2, 3


class Gather:
    def __init__(self, srcs, dsts, sems, local, ahead=2, lag=1):
        self.groups = gather_groups()
        self.srcs, self.dsts, self.sems = srcs, dsts, sems
        self.ahead, self.lag = ahead, lag
        clip, frame = lax.axis_index("clip"), lax.axis_index("frame")
        self.z, self.y, self.x, self.c = clip // 2, clip % 2, frame // 2, frame % 2
        z, y, x, c = self.z, self.y, self.x, self.c
        self.zpeers = [self.dev(lax.rem(z + k, 4), y, x, c) for k in (1, 2, 3)]
        self.ypeer, self.xpeer, self.cpeer = self.dev(z, 1 - y, x, c), self.dev(z, y, 1 - x, c), self.dev(z, y, x, 1 - c)
        self.moved = {k: {} for k in ("z", "y0", "y", "x1", "x2", "c1", "c2")}
        self.step = 0
        self.local = local

    @staticmethod
    def dev(z, y, x, c):
        return {"clip": z * 2 + y, "frame": x * 2 + c}

    def peers(self):
        return self.zpeers + [self.ypeer, self.xpeer, self.cpeer]

    def direct(self, g):
        return g < DIRECT

    def two(self, g):
        return self.span(g, 3 * self.c, 3) if self.direct(g) else self.span(g, 3 * self.c + self.x, 2)

    def span(self, g, first, count):
        _, _, _, r0, rows, unit, c0, width = self.groups[g]
        return pl.multiple_of(r0 + unit * first, 16), unit * count, c0, width

    def src(self, g, span):
        key, name, lead = self.groups[g][:3]
        r = self.srcs[name] if lead is None else self.srcs[name].at[lead]
        return r.at[pl.ds(span[0], span[1]), pl.ds(span[2], span[3])]

    def dst(self, g, z, y, span):
        key, name, lead = self.groups[g][:3]
        cs = pl.ds(span[2], span[3])
        r = self.dsts[name] if lead is None else self.dsts[name].at[lead]
        per = 384 if name == "o" else 96
        return r.at[pl.ds(pl.multiple_of((z * 2 + y) * per + span[0], 16), span[1]), cs]

    def remote(self, kind, i, s, d, peer):
        return pltpu.make_async_remote_copy(
            src_ref=s,
            dst_ref=d,
            send_sem=self.sems[0].at[kind + i],
            recv_sem=self.sems[1].at[kind + i],
            device_id=peer,
            device_id_type=MESH,
        )

    def relay(self, g, kind, items, span, peer):
        return Many(
            [self.remote(22 * g + kind, i, self.dst(g, zz, yy, span), self.dst(g, zz, yy, span), peer) for i, (zz, yy) in items]
        )

    def start_z(self, g):
        two = self.two(g)
        self.moved["z"][g] = Many(
            [self.remote(22 * g, k, self.src(g, two), self.dst(g, self.z, self.y, two), p) for k, p in enumerate(self.zpeers)]
        )
        self.moved["y0"][g] = Many([self.remote(22 * g, 3, self.src(g, two), self.dst(g, self.z, self.y, two), self.ypeer)])

    def begin(self):
        for g in range(self.ahead):
            self.start_z(g)

    def others(self, first):
        return [(q, lax.rem(self.z + q, 4)) for q in range(first, 4)]

    def tick(self):
        s, lag, ng, m, y = self.step, self.lag, len(self.groups), self.moved, self.y
        if s >= ng + 3 * lag:
            return False
        self.step += 1
        if s == 0:
            for cp in self.local:
                cp.wait()
        one, half = (3 * self.c + 2 * self.x, 1), (3 * self.c, 3)
        if s < ng:
            m["z"][s].wait_recv()
            if s + self.ahead < ng:
                self.start_z(s + self.ahead)
            m["y"][s] = self.relay(s, 4, [(q - 1, (zz, y)) for q, zz in self.others(1)], self.two(s), self.ypeer)
            if not self.direct(s):
                m["x1"][s] = self.relay(s, 7, [(q - 1, (zz, y)) for q, zz in self.others(1)], self.span(s, *one), self.xpeer)
        g = s - lag
        if 0 <= g < ng:
            m["y0"][g].wait_recv()
            m["y"][g].wait_recv()
            if not self.direct(g):
                m["x2"][g] = self.relay(g, 10, [(q, (zz, 1 - y)) for q, zz in self.others(0)], self.span(g, *one), self.xpeer)
                m["x1"][g].wait_recv()
            m["c1"][g] = self.relay(g, 14, [(q - 1, (zz, y)) for q, zz in self.others(1)], self.span(g, *half), self.cpeer)
        g = s - 2 * lag
        if 0 <= g < ng:
            if not self.direct(g):
                m["x2"][g].wait_recv()
            m["c2"][g] = self.relay(g, 17, [(q, (zz, 1 - y)) for q, zz in self.others(0)], self.span(g, *half), self.cpeer)
        g = s - 3 * lag
        if 0 <= g < ng:
            m["c1"][g].wait_recv()
            m["c2"][g].wait_recv()
        return True

    def need(self, key):
        last = max(i for i, g in enumerate(self.groups) if g[0] == key)
        while self.step <= last + 3 * self.lag:
            self.tick()

    def finish(self):
        while self.tick():
            pass
        for kind in self.moved.values():
            for cps in kind.values():
                cps.wait_send()


PIECES = [(i, 1) for i in range(6)] + [(6, 4), (10, 3), (13, 3)] + [(16 + i, 1) for i in range(4)] + [(20, 4)]


def piece_slots():
    for first, count in PIECES:
        for i in range(8 * count):
            yield first + i // 8, i % 8, i // count, first + i % count


def placement(part):
    row = iota((256, 1), 0)
    lane = row & 127
    return onehot(jnp.where(lane < 96, (2 * part + (row >> 7)) * 96 + lane, -1), D)


def place(rows):
    total = dg(rows(0), placement(0), 1, 0)
    for part in range(1, 4):
        total = total + dg(rows(part), placement(part), 1, 0)
    return total


def pick_rows(index):
    return jnp.where(iota((256, 128), 1) == index[...], 1.0, 0.0).astype(bf16)


BATCHES = ([3, 4, 5, 6, 7, 8, 9, 13, 14, 15, 18, 19, 20, 21, 22, 23], [0, 1, 2, 10, 11, 12, 16, 17])
PLACES = {p: i for i, p in enumerate(BATCHES[0] + BATCHES[1])}


class Reduce:
    def __init__(self, batch, blocks, work, received, result, nidx, sems):
        self.batch, self.blocks, self.work = batch, blocks, work
        self.received, self.result, self.nidx, self.sems = received, result, nidx, sems
        clip, frame = lax.axis_index("clip"), lax.axis_index("frame")
        self.clip, self.frame, self.x, self.c = clip, frame, frame // 2, frame % 2
        self.xpeer = {"clip": clip, "frame": (1 - self.x) * 2 + self.c}
        self.cpeer = {"clip": clip, "frame": self.x * 2 + 1 - self.c}
        self.width = len(BATCHES[batch]) * 32
        self.count = 0
        self.sent = []

    def lanes(self, quarter):
        return pl.ds(pl.multiple_of(2048 * self.batch + self.width * quarter, 128), self.width)

    def send(self, src, dst, peer):
        i = 16 * self.batch + self.count
        self.count += 1
        cp = pltpu.make_async_remote_copy(
            src_ref=src, dst_ref=dst, send_sem=self.sems.at[0, i], recv_sem=self.sems.at[1, i], device_id=peer, device_id_type=MESH
        )
        cp.start()
        self.sent.append(cp)
        return cp

    def add(self, first_row, quarter):
        ls = self.lanes(quarter)
        total = self.work[pl.ds(0, 256), ls].astype(f32) + self.work[pl.ds(first_row, 256), ls].astype(f32)
        self.work[pl.ds(0, 256), ls] = total.astype(bf16)

    def split(self):
        pieces = BATCHES[self.batch]
        for part in range(4):
            rows = self.blocks[pl.ds(512 * self.batch, 32 * len(pieces)), :]
            parts = dg(rows, placement(part), 1, 1).astype(bf16)
            for block, slot, owner, piece in piece_slots():
                if block in pieces and slot // 2 == part:
                    i = pieces.index(block)
                    tile = parts[32 * i : 32 * i + 32, 128 * (slot % 2) : 128 * (slot % 2) + 128]
                    self.work[pl.ds(32 * owner, 32), pl.ds(128 * PLACES[piece], 128)] = tile

    def over_cores(self):
        self.core = []
        for xx in range(2):
            ls = self.lanes(2 * xx + 1 - self.c)
            self.core.append(self.send(self.work.at[pl.ds(0, 256), ls], self.work.at[pl.ds(256, 256), ls], self.cpeer))

    def over_x(self):
        for xx in range(2):
            self.core[xx].wait_recv()
        for xx in range(2):
            self.add(256, 2 * xx + self.c)
        ls = self.lanes(2 * (1 - self.x) + self.c)
        self.across = self.send(self.work.at[pl.ds(0, 256), ls], self.work.at[pl.ds(512, 256), ls], self.xpeer)

    def to_owners(self):
        self.across.wait_recv()
        self.add(512, self.frame)
        ls = self.lanes(self.frame)
        self.here = pl.ds(512 * self.batch, self.width)
        mine = pl.ds(pl.multiple_of(32 * self.clip, 32), 32)
        self.received[mine, self.here] = self.work[mine, ls]
        self.owned = []
        for k in range(1, 8):
            j = lax.rem(self.clip + k, 8)
            rows = pl.ds(pl.multiple_of(32 * j, 32), 32)
            self.owned.append(
                self.send(self.work.at[rows, ls], self.received.at[mine, self.here], {"clip": j, "frame": self.frame})
            )

    def by_adapter(self):
        for cp in self.owned:
            cp.wait_recv()
        ls = self.lanes(self.frame)
        self.result[:, ls] = dg(pick_rows(self.nidx), self.received[:, self.here], 0, 0).astype(bf16)
        same = self.result.at[:, ls]
        self.back = [self.send(same, same, p) for p in (self.xpeer, self.cpeer)]

    def spread(self):
        self.back[0].wait_recv()
        same = self.result.at[:, self.lanes(2 * (1 - self.x) + self.c)]
        self.last = self.send(same, same, self.cpeer)

    def finish(self):
        self.back[1].wait_recv()
        self.last.wait_recv()
        for cp in self.sent:
            cp.wait_send()


def layer_kernel(
    gathers, hidx, x_ref, g_ref, hq, hp, hi, ho, had, hnm,
    out, ig, grads, spill,
    wq, wp, wi, wo, ad, nm, nbuf, nidx, received, rcv_a, rcv_b, big, x1, x2, tmp, o2, qkv2, a0, a1, us,
    wsem, ssem, rsem, psem, gssem, grsem, nsem, asem, bsem,
):
    buf_g, buf_d = big.at[0], big.at[1]

    clip = lax.axis_index("clip")
    me = lax.axis_index("frame")
    nf = 4
    peers = [lax.rem(me + k, nf) for k in range(1, nf)]

    fetch = [pltpu.make_async_copy(s, d, wsem.at[10 + i]) for i, (s, d) in enumerate(((x_ref, ig), (g_ref, out)))]
    for cp in fetch:
        cp.start()
    barrier = pltpu.get_barrier_semaphore()
    groups_of = [{"clip": clip, "frame": d} for d in peers]
    loads = {}
    if gathers:
        own = pl.ds(pl.multiple_of(clip * 96, 16), 96)
        local = [
            (hq.at[0], wq.at[0, own]), (hq.at[1], wq.at[1, own]), (hp.at[0], wp.at[0, own]), (hp.at[1], wp.at[1, own]),
            (hp.at[2], wp.at[2, own]), (hi, wi.at[own]), (ho, wo.at[pl.ds(pl.multiple_of(clip * 384, 16), 384)]),
            (had.at[:, cols(me * D, D)], big.at[0, pl.ds(256, 128), pl.ds(D, D)]), (hnm, nbuf.at[pl.ds(pl.multiple_of(clip * 16, 16), 16)]),
            (hidx, nidx.at[pl.ds(pl.multiple_of(clip * 32, 32), 32)]),
        ]
        local = [pltpu.make_async_copy(s, d, wsem.at[i]) for i, (s, d) in enumerate(local)]
        for cp in local:
            cp.start()
        net = Gather(
            {"q": hq, "p": hp, "i": hi, "o": ho},
            {"q": wq, "p": wp, "i": wi, "o": wo},
            (gssem, grsem),
            local[:7],
        )
        owners = [{"clip": lax.rem(clip + k, 8), "frame": me} for k in range(1, 8)]
        greet = groups_of + owners
    else:
        net = None
        for key, src, dst in (
            ("q0", hq.at[0], wq.at[0]), ("p0", hp.at[0], wp.at[0]), ("p1", hp.at[1], wp.at[1]), ("q1", hq.at[1], wq.at[1]),
            ("p2", hp.at[2], wp.at[2]), ("o", ho, wo), ("i", hi, wi), ("ad", had, ad), ("nm", hnm, nm),
        ):
            loads[key] = pltpu.make_async_copy(src, dst, wsem.at[len(loads)])
            loads[key].start()
        greet = groups_of
    for p in greet:
        pl.semaphore_signal(barrier, inc=1, device_id=p, device_id_type=MESH)
    pl.semaphore_wait(barrier, len(greet))

    def need(key, c=""):
        if net is not None:
            net.need(f"{key}{c}")
        elif not c:
            loads[key].wait()

    def need_tiles(key):
        def between(c):
            need(key, c)

        return between

    def tick():
        if net is not None:
            net.tick()

    if gathers:

        def to(peer, src, dst, sems, i):
            cp = pltpu.make_async_remote_copy(
                src_ref=src, dst_ref=dst, send_sem=sems.at[0, i], recv_sem=sems.at[1, i], device_id=peer, device_id_type=MESH
            )
            cp.start()
            return cp

        rows16 = pl.ds(pl.multiple_of(clip * 16, 16), 16)
        rows32 = pl.ds(pl.multiple_of(clip * 32, 32), 32)
        small = [to(p, hidx, nidx.at[rows32], nsem, k) for k, p in enumerate(owners)]
        small += [to(p, hnm, nbuf.at[rows16], nsem, 7 + k) for k, p in enumerate(owners)]
        net.begin()

    def exchange(step, src, index, rcv):
        sent = []
        for k, d in enumerate(peers):
            slot = pl.ds(k * GR, GR)
            o2[slot, :] = dg(onehot(index(d), R), src.get(), 1, 0).astype(bf16)
            cp = pltpu.make_async_remote_copy(
                src_ref=o2.at[slot],
                dst_ref=rcv.at[pl.ds(pl.multiple_of(me * GR, 16), GR)],
                send_sem=ssem.at[step, k],
                recv_sem=rsem.at[step, k],
                device_id={"clip": clip, "frame": d},
                device_id_type=MESH,
            )
            cp.start()
            sent.append(cp)
        rcv[pl.ds(pl.multiple_of(me * GR, 16), GR), :] = dg(onehot(index(me), R), src.get(), 1, 0).astype(bf16)

        def finish():
            for cp in sent:
                cp.wait_recv()
            for cp in sent:
                cp.wait_send()

        return finish

    def gain(k):
        return nm[k : k + 1, :]

    def norm(k, read, put):
        def body(rows):
            hat, _ = norm_rows(read(rows))
            put(rows, (hat * gain(k) + gain(3 + k)).astype(bf16))

        chunks(208, body)

    def rank(h, at, mask, m):
        us[:, pl.ds(32 * m, 32)] = jnp.where(mask, dg(h.get(), ad[:, pl.ds(at, h.width)], 1, 1), 0.0).astype(bf16)

    def forward(m, h, w, width, tile, mask, emit, between=None):
        rank(h, DOWN[m], mask, m)

        def body(c):
            acc = dg(h.get(), w[:, cols(c, tile)], 1, 0)
            acc = acc + dg(us[:, pl.ds(32 * m, 32)], ad[:, cols(UP[m] + c, tile)], 1, 0)
            emit(c, acc)

        tiles(width, tile, body, between)

    def rank_back(m, dz, mask):
        du = jnp.where(mask, dg(dz.get(), ad[:, pl.ds(UP[m], dz.width)], 1, 1), 0.0).astype(bf16)
        us[:, pl.ds(224, 32)] = du

    def backward(m, dz, w, width, tile, mask, emit, between=None):
        rank_back(m, dz, mask)
        backward_rows(m, dz, w, width, tile, emit, between)

    def backward_rows(m, dz, w, width, tile, emit, between=None):

        def body(c):
            acc = dg(dz.get(), w[cols(c, tile), :], 1, 1)
            acc = acc + dg(us[:, pl.ds(224, 32)], ad[:, cols(DOWN[m] + c, tile)], 1, 0)
            emit(c, acc)

        tiles(width, tile, body, between)

    def adapter_grads(m, h, dz):
        for at, side, rows in ((DOWN[m], 224, h), (UP[m], 32 * m, dz)):
            val = dg(us[:, pl.ds(side, 32)], rows.get(), 0, 0).astype(bf16)
            for k in range(rows.width // D):
                wo[pl.ds(32 * PLACES[at // D + k], 32), :] = val[:, k * D : k * D + D]

    p_a0, p_a1 = Part(a0, 0, D), Part(a1, 0, D)
    qkv1, h1 = Part(buf_g, 0, QKV), Part(buf_g, QKV, D)
    xt, o1, m1, spare = (Part(buf_d, D * i, D) for i in range(4))
    p_o2, p_qkv2, p_g, p_d = Part(o2, 0, D), Part(qkv2, 0, QKV), Part(buf_g, 0, FF), Part(buf_d, 0, FF)

    if gathers:
        def quarter_at(frame):
            if isinstance(frame, int):
                return 256 * (frame % 3), D * (frame // 3)
            return pl.multiple_of(256 * lax.rem(frame, 3), 32), pl.multiple_of(D * (frame // 3), 128)

        def quarter(frame, row, rows):
            r0, c0 = quarter_at(frame)
            return pl.ds(pl.multiple_of(r0 + row, 32), rows), pl.ds(c0, D)

        for cp in local[7:]:
            cp.wait()
        for cp in small[:7]:
            cp.wait_recv()
        side = pl.ds(D, D)
        big[0, pl.ds(384, 256), side] = dg(pick_rows(nidx), big[0, pl.ds(256, 128), side], 1, 0).astype(bf16)
        picked = []
        landing = quarter(me, 32 * clip, 32)
        for k, p in enumerate(owners):
            rows = pl.ds(pl.multiple_of(384 + 32 * p["clip"], 32), 32)
            picked.append(to(p, big.at[0, rows, side], big.at[(0,) + landing], asem, k))
        big[(0,) + landing] = big[0, pl.ds(pl.multiple_of(384 + 32 * clip, 32), 32), side]

    for i, (src, dst) in enumerate(((ig, a0), (out, a1))):
        fetch[i].wait()
        for g in range(4):
            dst[pl.ds(GR * g + 192, 16), :] = jnp.zeros((16, D), bf16)
            dst[pl.ds(GR * g, NP), :] = src[g // 2, g % 2]
        if dst is a0:
            arrive = exchange(0, p_a0, to_message, rcv_a)

    mask_t = clip_mask(392)
    mask_s = clip_mask(416)
    if gathers:
        tick()
        for cp in picked:
            cp.wait_recv()

        def block_of(frame):
            return big.at[(0,) + quarter(frame, 0, 256)]

        x, c = me // 2, me % 2
        xpeer, cpeer = {"clip": clip, "frame": (1 - x) * 2 + c}, {"clip": clip, "frame": x * 2 + 1 - c}
        picked.append(to(xpeer, block_of(me), block_of(me), asem, 7))
        picked.append(to(cpeer, block_of(me), block_of(me), asem, 8))
        for cp in small[7:]:
            cp.wait_recv()
        for j in range(8):
            qkv2[pl.ds(0, 16), pl.ds(j * 128, 128)] = nbuf[pl.ds(16 * j, 16), :]
        nm[...] = place(lambda part: qkv2[pl.ds(0, 16), pl.ds(256 * part, 256)])
    else:
        need("ad")
        need("nm")
    for _ in range(T1):
        tick()
    arrive()
    for i in range(4):
        xt.put(dg(onehot(to_patches(i), R), rcv_a[...], 1, 0).astype(bf16), pl.ds(i * GR, GR))
    norm(0, lambda rows: xt.get(rows).astype(f32), lambda rows, v: h1.put(v, rows))
    if gathers:
        picked[7].wait_recv()
        far = (1 - x) * 2 + c
        picked.append(to(cpeer, block_of(far), block_of(far), asem, 9))
        for _ in range(T2):
            tick()
        picked[8].wait_recv()
        picked[9].wait_recv()
        for cp in picked:
            cp.wait_send()
        for block, slot, owner, piece in piece_slots():
            r0, c0 = quarter_at(piece // 6)
            part = big[0, pl.ds(r0 + 32 * owner, 32), pl.ds(c0 + piece % 6 * 128, 128)]
            qkv2[pl.ds(block * 32, 32), pl.ds(slot * 128, 128)] = part
        joined = place(lambda part: qkv2[pl.ds(0, 768), pl.ds(256 * part, 256)]).astype(bf16)
        for block in range(24):
            ad[:, pl.ds(block * D, D)] = joined[block * 32 : block * 32 + 32]
    tick()
    forward(0, h1, wq.at[0], QKV, 768, mask_t, lambda c, acc: qkv1.put(acc.astype(bf16), off=c), need_tiles("q0"))
    tick()
    temporal_loop(lambda rows, n, bias, pairs: attend(qkv1, rows, n, bias, o1, pairs))
    tick()
    need("p0")
    forward(1, o1, wp.at[0], D, 384, mask_t, lambda c, acc: m1.put(acc.astype(bf16), off=c))
    tick()
    need("p1")
    forward(2, m1, wp.at[1], D, 384, mask_t, lambda c, acc: spare.put(acc.astype(bf16), off=c))
    tick()
    arrive = exchange(1, spare, from_patches, rcv_b)
    tick()
    saves = [pltpu.make_async_copy(b, spill.at[i], psem.at[i]) for i, b in enumerate((buf_g, buf_d))]
    for cp in saves:
        cp.start()
    for cp in saves:
        cp.wait()
    for _ in range(T3):
        tick()
    arrive()

    for g in range(4):
        rows = pl.ds(g * GR, GR)
        tb = dg(onehot(to_frames(g), R), rcv_b[...], 1, 0)
        x1[rows, :] = a0[rows, :].astype(f32) + tb
    tick()
    norm(1, lambda rows: x1[rows, :], lambda rows, v: p_o2.put(v, rows))
    tick()
    forward(3, p_o2, wq.at[1], QKV, 768, mask_s, lambda c, acc: p_qkv2.put(acc.astype(bf16), off=c), need_tiles("q1"))
    tick()
    spatial_loop(3, lambda rows, n, bias, pairs: attend(p_qkv2, rows, n, bias, p_o2, pairs))
    tick()
    need("p2")

    def add_spatial(c, acc):
        x2[:, cols(c, 384)] = x1[:, cols(c, 384)] + acc

    forward(4, p_o2, wp.at[2], D, 384, mask_s, add_spatial)
    tick()

    need("o")
    backward(6, p_a1, wo, FF, 768, mask_s, lambda c, acc: p_d.put(acc.astype(bf16), off=c), lambda c: tick())
    us[:, pl.ds(256, 32)] = us[:, pl.ds(224, 32)]

    norm(2, lambda rows: x2[rows, :], lambda rows, v: p_a0.put(v, rows))

    def activate(c, acc):
        tmp_w = acc.shape[1]
        tmp[:, pl.ds(0, tmp_w)] = acc
        @pl.loop(0, R // 32)
        def _(i):
            rows = pl.ds(pl.multiple_of(i * 32, 32), 32)
            v = tmp[rows, pl.ds(0, tmp_w)]
            phi, e = normal_parts(v)
            slope = phi + v * e * 0.3989422804014327
            p_g.put((v * phi).astype(bf16), rows, c)
            p_d.put((p_d.get(rows, c, tmp_w).astype(f32) * slope).astype(bf16), rows, c)

    forward(5, p_a0, wi, FF, 768, mask_s, activate, need_tiles("i"))

    def emit_out(c, acc):
        y = (x2[:, cols(c, 384)] + acc).astype(bf16)
        for g in range(4):
            out[g // 2, g % 2, :, cols(c, 384)] = y[g * GR : g * GR + NP]

    forward(6, p_g, wo, D, 384, mask_s, emit_out)
    if gathers:
        net.finish()
        for cp in small:
            cp.wait_send()

    us[:, pl.ds(224, 32)] = us[:, pl.ds(256, 32)]
    adapter_grads(6, p_g, p_a1)

    def emit_tmp(c, acc):
        tmp[:, cols(c, 384)] = acc

    backward(5, p_d, wi, D, 384, mask_s, emit_tmp)
    adapter_grads(5, p_a0, p_d)
    loads_back = [pltpu.make_async_copy(spill.at[i], b, psem.at[i]) for i, b in enumerate((buf_g, buf_d))]
    for cp in loads_back:
        cp.start()

    def step_two(rows):
        dx = a1[rows, :].astype(f32) + norm_back_rows(x2[rows, :], gain(2), tmp[rows, :])
        x2[rows, :] = dx
        a0[rows, :] = dx.astype(bf16)

    chunks(208, step_two)

    backward(4, p_a0, wp.at[2], D, 384, mask_s, lambda c, acc: p_a1.put(acc.astype(bf16), off=c))
    adapter_grads(4, p_o2, p_a0)
    spatial_loop(2, lambda rows, n, bias, pairs: attend_back(p_qkv2, rows, n, bias, p_a1, pairs, False))
    backward(3, p_qkv2, wq.at[1], D, 384, mask_s, emit_tmp)

    def step_one(rows):
        dx = x2[rows, :] + norm_back_rows(x1[rows, :], gain(1), tmp[rows, :])
        x2[rows, :] = dx
        a0[rows, :] = dx.astype(bf16)

    chunks(208, step_one)
    arrive = exchange(2, p_a0, to_message, rcv_a)
    norm(1, lambda rows: x1[rows, :], lambda rows, v: p_a1.put(v, rows))
    adapter_grads(3, p_a1, p_qkv2)
    if gathers:
        first, second = (Reduce(i, wo, wi, received, grads, nidx, bsem) for i in range(2))
        first.split()
    for cp in loads_back:
        cp.wait()
    arrive()

    if gathers:
        first.over_cores()
    for i in range(4):
        p_a0.put(dg(onehot(to_patches(i), R), rcv_a[...], 1, 0).astype(bf16), pl.ds(i * GR, GR))
    backward(2, p_a0, wp.at[1], D, 384, mask_t, lambda c, acc: p_a1.put(acc.astype(bf16), off=c))
    adapter_grads(2, m1, p_a0)
    if gathers:
        first.over_x()
    backward(1, p_a1, wp.at[0], D, 384, mask_t, lambda c, acc: spare.put(acc.astype(bf16), off=c))
    adapter_grads(1, o1, p_a1)
    temporal_loop(lambda rows, n, bias, pairs: attend_back(qkv1, rows, n, bias, spare, pairs, True))
    if gathers:
        first.to_owners()
    rank_back(0, qkv1, mask_t)
    adapter_grads(0, h1, qkv1)
    if gathers:
        second.split()
        second.over_cores()
        first.by_adapter()
    backward_rows(0, qkv1, wq.at[0], D, 384, emit_tmp)
    if gathers:
        second.over_x()
        first.spread()

    def step_zero(rows):
        dx = norm_back_rows(xt.get(rows).astype(f32), gain(0), tmp[rows, :])
        a0[rows, :] = dx.astype(bf16)

    chunks(208, step_zero)
    if gathers:
        second.to_owners()
    arrive = exchange(3, p_a0, from_patches, rcv_b)
    if gathers:
        second.by_adapter()
        first.finish()
        second.spread()
    arrive()
    for g in range(4):
        dxt = dg(onehot(to_frames(g), R), rcv_b[...], 1, 0)
        total = x2[pl.ds(g * GR, GR), :] + dxt
        ig[g // 2, g % 2] = total.astype(bf16)[:NP]
    if gathers:
        second.finish()
    else:
        for block in range(24):
            grads[:, pl.ds(block * D, D)] = wo[pl.ds(32 * PLACES[block], 32), :]


def layer(gathers, index_rows, x, g, hq, hp, hi, ho, ad, nm):
    vm = pl.BlockSpec(memory_space=pltpu.VMEM)
    hbm = pl.BlockSpec(memory_space=pl.ANY)
    dma = pltpu.SemaphoreType.DMA
    rows = lambda w, t=bf16: pltpu.VMEM((R, w), t)
    ng = len(gather_groups()) if gathers else 1
    return pl.pallas_call(
        functools.partial(layer_kernel, gathers),
        out_shape=[
            jax.ShapeDtypeStruct(x.shape, bf16),
            jax.ShapeDtypeStruct(x.shape, bf16),
            jax.ShapeDtypeStruct((128, 24 * 128) if gathers else (32, ADW), bf16),
            jax.ShapeDtypeStruct((2, R, FF), bf16),
        ],
        in_specs=[hbm] * 9,
        out_specs=[vm] * 3 + [hbm],
        scratch_shapes=[
            pltpu.VMEM((2, D, QKV), bf16), pltpu.VMEM((3, D, D), bf16), pltpu.VMEM((D, FF), bf16), pltpu.VMEM((FF, D), bf16),
            pltpu.VMEM((32, ADW), bf16), pltpu.VMEM((16, D), f32), pltpu.VMEM((128, 128), bf16),
            pltpu.VMEM((256, 128), jnp.int32), pltpu.VMEM((256, D), bf16),
            rows(D), rows(D), pltpu.VMEM((2, R, FF), bf16), rows(D, f32), rows(D, f32), rows(D, f32),
            rows(D), rows(QKV), rows(D), rows(D), rows(384),
            dma((12,)), dma((4, 3)), dma((4, 3)), dma((2,)), dma((22 * ng,)), dma((22 * ng,)), dma((2, 14)), dma((2, 10)), dma((2, 32)),
        ],
        compiler_params=pltpu.CompilerParams(
            collective_id=1, has_side_effects=True, vmem_limit_bytes=64 * 2**20 - 2**17
        ),
        name="layer",
    )(index_rows, x, g, hq, hp, hi, ho, ad, nm)


def piece_widths(w):
    return [w] * 6 + [4 * w] + [3 * w] * 2 + [w] * 4 + [4 * w]


def pack_adapters(adapt_down, adapt_down_wide, adapt_up_qkv, adapt_up, adapt_up_wide):
    adapters = adapt_down_wide.shape[0]

    def flat(v):
        return v.reshape(adapters, RANK, -1)

    return jnp.concatenate(
        [
            flat(adapt_down.transpose(1, 3, 0, 2)),
            flat(adapt_down_wide.transpose(0, 2, 1)),
            flat(adapt_up_qkv.transpose(1, 2, 0, 3)),
            flat(adapt_up.transpose(1, 2, 0, 3)),
            flat(adapt_up_wide),
        ],
        axis=-1,
    )


def join_pieces(parts, w):
    joined, at = [], 0
    for width in piece_widths(w):
        piece = parts[:, :, at : at + width]
        joined.append(piece.transpose(1, 0, 2).reshape(parts.shape[1], -1))
        at += width
    return jnp.concatenate(joined, axis=-1)


def split_pieces(rows, w, owners):
    parts, at = [], 0
    for width in piece_widths(w):
        piece = rows[:, at : at + width * owners]
        parts.append(piece.reshape(rows.shape[0], owners, width).transpose(1, 0, 2))
        at += width * owners
    return jnp.concatenate(parts, axis=-1)


def per_device(
    inputs,
    out_grad,
    adapter_index,
    norm_gain,
    norm_bias,
    qkv_weight,
    proj_weight,
    mlp_in,
    mlp_out,
    adapt_down,
    adapt_down_wide,
    adapt_up_qkv,
    adapt_up,
    adapt_up_wide,
):
    owners = lax.axis_size("clip")
    adapters = adapt_down_wide.shape[0]
    clips = inputs.shape[0]
    w = norm_gain.shape[1]
    packed = pack_adapters(adapt_down, adapt_down_wide, adapt_up_qkv, adapt_up, adapt_up_wide)
    norms = jnp.concatenate([norm_gain, norm_bias], axis=0)
    if owners == 8:
        index_rows = adapter_index[:, None] * RANK + jnp.arange(RANK, dtype=jnp.int32)[None, :]
        index_rows = jnp.broadcast_to(index_rows.reshape(clips * RANK, 1), (clips * RANK, 128))
        pieces = packed.reshape(adapters * RANK, 24, w)
        table = jnp.pad(pieces, ((0, 0), (0, 0), (0, 128 - w))).reshape(adapters * RANK, 24 * 128)
        own_norms = jnp.pad(norms, ((0, 10), (0, 128 - w)))
        output, input_grad, grads, _ = layer(
            True, index_rows, inputs, out_grad, qkv_weight, proj_weight, mlp_in, mlp_out, table, own_norms
        )
        grads = grads.reshape(adapters, RANK, 24, 128)[..., :w].astype(f32)
        summed = jnp.concatenate([grads[:, :, PLACES[p]] for p in range(24)], axis=-1)
    else:
        full_qkv = lax.all_gather(qkv_weight, "clip", axis=1, tiled=True)
        full_proj = lax.all_gather(proj_weight, "clip", axis=1, tiled=True)
        full_in = lax.all_gather(mlp_in, "clip", axis=0, tiled=True)
        full_out = lax.all_gather(mlp_out, "clip", axis=0, tiled=True)
        table = lax.all_gather(packed, "clip", axis=0)
        all_norms = lax.all_gather(norms, "clip", axis=0)
        nm = jnp.pad(all_norms.transpose(1, 0, 2).reshape(6, D).astype(f32), ((0, 10), (0, 0)))
        chosen = jnp.take(table, adapter_index, axis=1).reshape(owners, clips * RANK, 24 * w)
        ad = join_pieces(chosen, w)
        output, input_grad, grads, _ = layer(
            False, adapter_index, inputs, out_grad, full_qkv, full_proj, full_in, full_out, ad, nm
        )
        parts = split_pieces(grads, w, owners)
        parts = lax.all_to_all(parts, "clip", split_axis=0, concat_axis=0, tiled=True)
        every = lax.all_gather(adapter_index, "clip", axis=0, tiled=True)
        pick = (every[:, None] == jnp.arange(adapters, dtype=jnp.int32)[None, :]).astype(bf16)
        summed = jnp.einsum(
            "ca,crm->arm", pick, parts.reshape(owners * clips, RANK, 24 * w), preferred_element_type=f32
        )
        summed = lax.psum(summed.astype(bf16), "frame").astype(f32)
    return (output, input_grad) + unpack_grads(summed, w)


def unpack_grads(summed, w):
    adapters = summed.shape[0]
    down = summed[:, :, : 6 * w].reshape(adapters, RANK, 6, w).transpose(2, 0, 3, 1)
    down_wide = summed[:, :, 6 * w : 10 * w].transpose(0, 2, 1)
    up_qkv = summed[:, :, 10 * w : 16 * w].reshape(adapters, RANK, 2, 3 * w).transpose(2, 0, 1, 3)
    up = summed[:, :, 16 * w : 20 * w].reshape(adapters, RANK, 4, w).transpose(2, 0, 1, 3)
    return (down, down_wide, up_qkv, up, summed[:, :, 20 * w :])


def solution(mesh):
    return jax.shard_map(
        per_device,
        mesh=mesh,
        in_specs=(
            P("clip", "frame", None, None),
            P("clip", "frame", None, None),
            P("clip"),
            P(None, "clip"),
            P(None, "clip"),
            P(None, "clip", None),
            P(None, "clip", None),
            P("clip", None),
            P("clip", None),
            P(None, None, "clip", None),
            P(None, "clip", None),
            P(None, None, None, "clip"),
            P(None, None, None, "clip"),
            P(None, None, "clip"),
        ),
        out_specs=(
            P("clip", "frame", None, None),
            P("clip", "frame", None, None),
            P(None, None, "clip", None),
            P(None, "clip", None),
            P(None, None, None, "clip"),
            P(None, None, None, "clip"),
            P(None, None, "clip"),
        ),
        check_vma=False,
    )
```

profile of v0, /device:TPU:0, one launch (start us, length us, event | category | flops | bytes accessed | tf_op | source)
XLA Modules:
  0.0 302.6 jit_solution(8847234757181074182)
XLA Ops:
  0.6 0.0 copy-start.6
  0.6 0.0 copy-start.5
  0.7 0.0 copy-start.4
  0.7 0.7 broadcast_multiply_fusion
  1.4 0.1 iota_add_fusion
  1.5 0.1 add.27
  1.5 1.3 fusion.5.hnm
  2.8 0.7 broadcast_in_dim.2.hidx
  3.5 1.0 copy.29
  4.5 0.1 reshape.76
  4.7 1.1 copy.28
  5.8 0.2 reshape.75
  6.0 0.0 copy-done.4
  6.0 0.1 copy.27
  6.1 0.2 reshape.74
  6.3 0.0 copy-done.6
  6.3 0.0 copy-done.5
  6.3 0.4 concatenate.27
  6.7 1.2 reshape.77
  7.9 0.0 copy-start.1
  7.9 0.2 pad.8
  8.1 1.0 copy.42
  9.1 0.0 copy-start.2
  9.1 0.1 copy-done.1
  9.3 1.1 copy.30.x_ref
  10.4 0.3 copy-done.2
  10.7 1.2 copy.31.g_ref
  11.9 281.1 %layer.1 = (bf16[2,2,196,768]{3,2,1,0:T(8,128)(2,1)}, bf16[2,2,196,768]{3,2,1,0:T(8,128)(2,1)}, bf16[128,3072]{1,0:T(8,128)(2,1)}, bf16[2,832,3072]{2,1,0:T(8,128)(2,1)}) custom-call(s32[32,128]{1,0:T(8,128)} %broadcast_in_dim.2.hidx, bf16[2,2,196,768]{3,2,1,0:T(8,128)(2,1)} %copy.30.x_ref, bf16[2,2,196,768]{3,2,1,0:T(8,128)(2,1)} %copy.31.g_ref, ...), custom_call_target="tpu_custom_call" | custom-call | tf_op jit(solution)/shard_map/layer/pallas_call | solution.py:863
  292.9 0.0 copy-start.3
  292.9 3.3 %copy.34 = bf16[2,2,196,768]{3,1,2,0:T(2,128)(2,1)} copy(bf16[2,2,196,768]{3,2,1,0:T(8,128)(2,1)} %get-tuple-element.20) | data formatting | bytes 2408448
  296.2 0.0 copy-done.3
  296.2 0.2 copy.38
  296.4 0.2 copy_convert_fusion
  296.6 0.7 maximum_bitcast_fusion.1
  297.4 0.1 slice_bitcast_fusion.3
  297.5 1.0 maximum_bitcast_fusion.2
  298.4 0.8 maximum_bitcast_fusion
  299.2 0.0 copy-start
  299.2 0.2 concatenate.31
  299.4 0.3 reshape.80
  299.7 0.8 copy.43
  300.5 0.0 copy-done
  300.5 1.9 copy.35
  (2 shorter events, 0.0 us)
Async XLA Ops:
  0.6 5.7 %copy-start.6 = (bf16[8,16,384]{2,1,0:T(8,128)(2,1)S(1)}, bf16[8,16,384]{2,1,0:T(8,128)(2,1)}, u32[]{:S(2)}) copy-start(bf16[8,16,384]{2,1,0:T(8,128)(2,1)} %param.27) | copy-start | bytes 294916
  0.6 5.7 %copy-start.5 = (bf16[8,384,16]{1,2,0:T(8,128)(2,1)S(1)}, bf16[8,384,16]{1,2,0:T(8,128)(2,1)}, u32[]{:S(2)}) copy-start(bf16[8,384,16]{1,2,0:T(8,128)(2,1)} %param.24) | copy-start | bytes 294916
  0.7 5.3 %copy-start.4 = (bf16[6,8,96,16]{2,3,1,0:T(8,128)(2,1)S(1)}, bf16[6,8,96,16]{2,3,1,0:T(8,128)(2,1)}, u32[]{:S(2)}) copy-start(bf16[6,8,96,16]{2,3,1,0:T(8,128)(2,1)} %param.23) | copy-start | bytes 442372
  7.9 1.3 copy-start.1
  9.1 1.5 copy-start.2
  292.9 3.3 %copy-start.3 = (bf16[128,3072]{1,0:T(8,128)(2,1)S(1)}, bf16[128,3072]{1,0:T(8,128)(2,1)}, u32[]{:S(2)}) copy-start(bf16[128,3072]{1,0:T(8,128)(2,1)} %get-tuple-element.12) | copy-start | bytes 2359300
  299.2 1.3 copy-start
where the time goes:
time: 308 us; the launch traced here: 303 us
  Pallas kernels  281 us (91%)
  local copies, waits for them, and re-layouts  15.8 us (5%)
  other arithmetic  4.75 us (2%)
    pallas_call x1, Pallas kernels, layer(): pl.pallas_call(functools.partial(layer_kernel, gathers), out_shape=[jax.S...  281 us
    unnamed x20, local copies, waits for them, and re-layouts  9.24 us

commit v1 on v0

--- a/solution.py
+++ b/solution.py
@@ -700,10 +700,10 @@
     temporal_loop(lambda rows, n, bias, pairs: attend(qkv1, rows, n, bias, o1, pairs))
     tick()
     need("p0")
-    forward(1, o1, wp.at[0], D, 384, mask_t, lambda c, acc: m1.put(acc.astype(bf16), off=c))
+    forward(1, o1, wp.at[0], D, 256, mask_t, lambda c, acc: m1.put(acc.astype(bf16), off=c))
     tick()
     need("p1")
-    forward(2, m1, wp.at[1], D, 384, mask_t, lambda c, acc: spare.put(acc.astype(bf16), off=c))
+    forward(2, m1, wp.at[1], D, 256, mask_t, lambda c, acc: spare.put(acc.astype(bf16), off=c))
     tick()
     arrive = exchange(1, spare, from_patches, rcv_b)
     tick()
@@ -730,9 +730,9 @@
     need("p2")
 
     def add_spatial(c, acc):
-        x2[:, cols(c, 384)] = x1[:, cols(c, 384)] + acc
-
-    forward(4, p_o2, wp.at[2], D, 384, mask_s, add_spatial)
+        x2[:, cols(c, 256)] = x1[:, cols(c, 256)] + acc
+
+    forward(4, p_o2, wp.at[2], D, 256, mask_s, add_spatial)
     tick()
 
     need("o")
@@ -756,11 +756,11 @@
     forward(5, p_a0, wi, FF, 768, mask_s, activate, need_tiles("i"))
 
     def emit_out(c, acc):
-        y = (x2[:, cols(c, 384)] + acc).astype(bf16)
+        y = (x2[:, cols(c, 256)] + acc).astype(bf16)
         for g in range(4):
-            out[g // 2, g % 2, :, cols(c, 384)] = y[g * GR : g * GR + NP]
-
-    forward(6, p_g, wo, D, 384, mask_s, emit_out)
+            out[g // 2, g % 2, :, cols(c, 256)] = y[g * GR : g * GR + NP]
+
+    forward(6, p_g, wo, D, 256, mask_s, emit_out)
     if gathers:
         net.finish()
         for cp in small:
@@ -770,9 +770,9 @@
     adapter_grads(6, p_g, p_a1)
 
     def emit_tmp(c, acc):
-        tmp[:, cols(c, 384)] = acc
-
-    backward(5, p_d, wi, D, 384, mask_s, emit_tmp)
+        tmp[:, cols(c, 256)] = acc
+
+    backward(5, p_d, wi, D, 256, mask_s, emit_tmp)
     adapter_grads(5, p_a0, p_d)
     loads_back = [pltpu.make_async_copy(spill.at[i], b, psem.at[i]) for i, b in enumerate((buf_g, buf_d))]
     for cp in loads_back:
@@ -785,10 +785,10 @@
 
     chunks(208, step_two)
 
-    backward(4, p_a0, wp.at[2], D, 384, mask_s, lambda c, acc: p_a1.put(acc.astype(bf16), off=c))
+    backward(4, p_a0, wp.at[2], D, 256, mask_s, lambda c, acc: p_a1.put(acc.astype(bf16), off=c))
     adapter_grads(4, p_o2, p_a0)
     spatial_loop(2, lambda rows, n, bias, pairs: attend_back(p_qkv2, rows, n, bias, p_a1, pairs, False))
-    backward(3, p_qkv2, wq.at[1], D, 384, mask_s, emit_tmp)
+    backward(3, p_qkv2, wq.at[1], D, 256, mask_s, emit_tmp)
 
     def step_one(rows):
         dx = x2[rows, :] + norm_back_rows(x1[rows, :], gain(1), tmp[rows, :])
@@ -810,11 +810,11 @@
         first.over_cores()
     for i in range(4):
         p_a0.put(dg(onehot(to_patches(i), R), rcv_a[...], 1, 0).astype(bf16), pl.ds(i * GR, GR))
-    backward(2, p_a0, wp.at[1], D, 384, mask_t, lambda c, acc: p_a1.put(acc.astype(bf16), off=c))
+    backward(2, p_a0, wp.at[1], D, 256, mask_t, lambda c, acc: p_a1.put(acc.astype(bf16), off=c))
     adapter_grads(2, m1, p_a0)
     if gathers:
         first.over_x()
-    backward(1, p_a1, wp.at[0], D, 384, mask_t, lambda c, acc: spare.put(acc.astype(bf16), off=c))
+    backward(1, p_a1, wp.at[0], D, 256, mask_t, lambda c, acc: spare.put(acc.astype(bf16), off=c))
     adapter_grads(1, o1, p_a1)
     temporal_loop(lambda rows, n, bias, pairs: attend_back(qkv1, rows, n, bias, spare, pairs, True))
     if gathers:
@@ -825,7 +825,7 @@
         second.split()
         second.over_cores()
         first.by_adapter()
-    backward_rows(0, qkv1, wq.at[0], D, 384, emit_tmp)
+    backward_rows(0, qkv1, wq.at[0], D, 256, emit_tmp)
     if gathers:
         second.over_x()
         first.spread()

time: 308 us -> 304 us (0.987)
  Pallas kernels: 281 us -> 277 us
    pallas_call x1, Pallas kernels: 281 us -> 277 us  [layer(): pl.pallas_call(functools.partial(layer_kernel, gathers), out_shape=[jax.S...]
where the time goes in v1:
time: 304 us; the launch traced here: 299 us
  Pallas kernels  277 us (91%)
  local copies, waits for them, and re-layouts  15.8 us (5%)
  other arithmetic  4.75 us (2%)
    pallas_call x1, Pallas kernels, layer(): pl.pallas_call(functools.partial(layer_kernel, gathers), out_shape=[jax.S...  277 us
    unnamed x20, local copies, waits for them, and re-layouts  9.24 us

profile of v1, /device:TPU:0, one launch (start us, length us, event | category | flops | bytes accessed | tf_op | source)
XLA Modules:
  0.0 298.6 jit_solution(97418369596051519)
XLA Ops:
  0.6 0.0 copy-start.6
  0.6 0.0 copy-start.5
  0.7 0.0 copy-start.4
  0.7 0.7 broadcast_multiply_fusion
  1.4 0.1 iota_add_fusion
  1.5 0.1 add.27
  1.5 1.3 fusion.5.hnm
  2.8 0.7 broadcast_in_dim.2.hidx
  3.5 1.0 copy.29
  4.5 0.1 reshape.76
  4.7 1.1 copy.28
  5.8 0.2 reshape.75
  6.0 0.0 copy-done.4
  6.0 0.1 copy.27
  6.1 0.2 reshape.74
  6.3 0.0 copy-done.6
  6.3 0.0 copy-done.5
  6.3 0.4 concatenate.27
  6.7 1.2 reshape.77
  7.9 0.0 copy-start.1
  7.9 0.2 pad.8
  8.1 1.0 copy.42
  9.1 0.0 copy-start.2
  9.1 0.1 copy-done.1
  9.3 1.1 copy.30.x_ref
  10.4 0.3 copy-done.2
  10.7 1.2 copy.31.g_ref
  11.9 276.8 %layer.1 = (bf16[2,2,196,768]{3,2,1,0:T(8,128)(2,1)}, bf16[2,2,196,768]{3,2,1,0:T(8,128)(2,1)}, bf16[128,3072]{1,0:T(8,128)(2,1)}, bf16[2,832,3072]{2,1,0:T(8,128)(2,1)}) custom-call(s32[32,128]{1,0:T(8,128)} %broadcast_in_dim.2.hidx, bf16[2,2,196,768]{3,2,1,0:T(8,128)(2,1)} %copy.30.x_ref, bf16[2,2,196,768]{3,2,1,0:T(8,128)(2,1)} %copy.31.g_ref, ...), custom_call_target="tpu_custom_call" | custom-call | tf_op jit(solution)/shard_map/layer/pallas_call | solution.py:863
  288.6 0.0 copy-start.3
  288.6 3.3 %copy.34 = bf16[2,2,196,768]{3,1,2,0:T(2,128)(2,1)} copy(bf16[2,2,196,768]{3,2,1,0:T(8,128)(2,1)} %get-tuple-element.20) | data formatting | bytes 2408448
  291.9 0.0 copy-done.3
  291.9 0.2 copy.38
  292.1 0.2 copy_convert_fusion
  292.3 0.7 maximum_bitcast_fusion.1
  293.1 0.1 slice_bitcast_fusion.3
  293.1 1.0 maximum_bitcast_fusion.2
  294.1 0.8 maximum_bitcast_fusion
  294.9 0.0 copy-start
  294.9 0.2 concatenate.31
  295.1 0.3 reshape.80
  295.4 0.8 copy.43
  296.2 0.0 copy-done
  296.2 1.9 copy.35
  (2 shorter events, 0.0 us)
Async XLA Ops:
  0.6 5.7 %copy-start.6 = (bf16[8,16,384]{2,1,0:T(8,128)(2,1)S(1)}, bf16[8,16,384]{2,1,0:T(8,128)(2,1)}, u32[]{:S(2)}) copy-start(bf16[8,16,384]{2,1,0:T(8,128)(2,1)} %param.27) | copy-start | bytes 294916
  0.6 5.7 %copy-start.5 = (bf16[8,384,16]{1,2,0:T(8,128)(2,1)S(1)}, bf16[8,384,16]{1,2,0:T(8,128)(2,1)}, u32[]{:S(2)}) copy-start(bf16[8,384,16]{1,2,0:T(8,128)(2,1)} %param.24) | copy-start | bytes 294916
  0.7 5.3 %copy-start.4 = (bf16[6,8,96,16]{2,3,1,0:T(8,128)(2,1)S(1)}, bf16[6,8,96,16]{2,3,1,0:T(8,128)(2,1)}, u32[]{:S(2)}) copy-start(bf16[6,8,96,16]{2,3,1,0:T(8,128)(2,1)} %param.23) | copy-start | bytes 442372
  7.9 1.3 copy-start.1
  9.1 1.5 copy-start.2
  288.6 3.3 %copy-start.3 = (bf16[128,3072]{1,0:T(8,128)(2,1)S(1)}, bf16[128,3072]{1,0:T(8,128)(2,1)}, u32[]{:S(2)}) copy-start(bf16[128,3072]{1,0:T(8,128)(2,1)} %get-tuple-element.12) | copy-start | bytes 2359300
  294.9 1.3 copy-start
